TPU v7x, 256 devices: a whole 4x4x8 slice. The times are simulated.
256 devices in a mesh: lon: 32 (over z, y), lat: 4 (over x), dep: 2 (over core).
Axes of the slice: x: 4, y: 4, z: 8, core: 2. Of those that a mesh axis runs over, the one named last changes fastest.
Arguments:
- adjoint_u: float32 [64, 128, 4096], P('dep', 'lat', 'lon'), may hold values from -6 to 6
- adjoint_v: float32 [64, 128, 4096], P('dep', 'lat', 'lon'), may hold values from -6 to 6
- adjoint_t: float32 [64, 128, 4096], P('dep', 'lat', 'lon'), may hold values from -6 to 6
- zonal_vel: float32 [64, 128, 4096], P('dep', 'lat', 'lon'), may hold values from -1.5 to 1.5
- merid_vel: float32 [64, 128, 4096], P('dep', 'lat', 'lon'), may hold values from -1.5 to 1.5
- coriolis_dt: float32 [128], P('lat'), may hold values from -0.8 to 0.8
- layer_thick: float32 [64], P('dep'), may hold values from 0.5 to 2
- overturn_weight: float32 [64, 128], P(None, 'lat'), may hold values from 0.3 to 3
- overturn_target: float32 [64, 128], P(None, 'lat'), may hold values from -5 to 5
- atlantic: int32 [128, 4096], P('lat', 'lon'), may hold values from 0 to 1, as said below
- bottom_level: int32 [128, 4096], P('lat', 'lon'), may hold values from 0 to 64
Outputs:
- result_u: float32 [64, 128, 4096], P('dep', 'lat', 'lon')
- result_v: float32 [64, 128, 4096], P('dep', 'lat', 'lon')
- result_t: float32 [64, 128, 4096], P('dep', 'lat', 'lon')
Inputs may be any that keep to these rules, and one draw needn't show every extreme that they name: `atlantic`: in each latitude row the basin is one run of consecutive longitudes, possibly continuing across the seam at longitude 0. `bottom_level`: 0 marks land.
All inputs are finite; a program needn't handle non-finite values.
Results may differ from a plain program's by a relative error of at most 0.00002.
Values sent between devices are 32-bit elements; how exact they have to be, the bound alone decides.
A program may use at most 64 MiB of HBM per device.

v0:
```python
import jax
import jax.numpy as jnp
from jax import lax
from jax.experimental import pallas as pl
from jax.experimental.pallas import tpu as pltpu
from jax.sharding import PartitionSpec as P

MESH = pl.DeviceIdType.MESH
F32 = jnp.float32
HALO = 8
OWN = 32
ROWS = OWN + 2 * HALO
NLON, NLAT, NDEP = 32, 4, 2
RING_Y, RING_Z = 4, 8
T, V, VV, UU, U = range(5)


def lanes():
    return lax.broadcasted_iota(jnp.int32, (8, 128), 1)


def sublanes():
    return lax.broadcasted_iota(jnp.int32, (8, 128), 0)


def lroll(x, shift):
    shift = shift % 128
    return x if shift == 0 else pltpu.roll(x, shift, 1)


def sroll(x, shift):
    return pltpu.roll(x, shift % 8, 0)


def pack(tiles):
    at = (lanes() + 8) // 32 % 4
    joined = tiles[0]
    for g in range(1, 4):
        joined = jnp.where(at == g, lroll(tiles[g], 32 * g), joined)
    return jnp.where(lanes() % 32 < 16, lroll(joined, 8), lroll(joined, 24))


def merge(own, left, right):
    place = lanes() % 32
    return jnp.where(
        place < 8, lroll(left, -16), jnp.where(place >= 24, lroll(right, 16), own)
    )


def spread(strip):
    return jnp.where(lanes() % 32 < 16, lroll(strip, -8), lroll(strip, -24))


def suffix_tile(x):
    lane, sub = lanes(), sublanes()
    for k in (1, 2, 4):
        x = x + jnp.where(sub < 8 - k, sroll(x, -k), 0.0)
    group = jnp.broadcast_to(x[0:1, :], (8, 128))
    out, total = x, group
    for j in (1, 2, 3):
        moved = lroll(group, -32 * j)
        out = out + jnp.where(lane < 128 - 32 * j, moved, 0.0)
        total = total + moved
    return out, total


def prefix_tile(x):
    lane, sub = lanes(), sublanes()
    for k in (1, 2, 4):
        x = x + jnp.where(sub >= k, sroll(x, k), 0.0)
    group = jnp.broadcast_to(x[7:8, :], (8, 128))
    out, total = x, group
    for j in (1, 2, 3):
        moved = lroll(group, 32 * j)
        out = out + jnp.where(lane >= 32 * j, moved, 0.0)
        total = total + moved
    return out, total


def by_rows(low, high, block, fn):
    def body(n, c):
        stores = []
        for r in range(block):
            stores += fn(low + block * n + r)
        for ref, index, value in stores:
            ref[index] = value
        return c

    lax.fori_loop(0, (high - low) // block, body, 0)


def reduce_lanes(make):
    lane = lanes()

    def tree(level, start):
        if level < 0:
            return make(start)
        step = 1 << level
        a = tree(level - 1, start)
        b = tree(level - 1, start + step)
        even = (lane & step) == 0
        return jnp.where(even, a, b) + lroll(jnp.where(even, b, a), -step)

    return tree(6, 0)


def kernel(
    adj_u, adj_v, adj_t, zonal, merid, cor, thick, weight_t, target_t, atl, bottom,
    out_u, out_v, out_t,
    raw, tr, uu, vv, mask, strips_own, strips_l, strips_r, s_raw, s_mask, s_tr, s_edge,
    flat, coef, flat_own, flat_l, flat_r, flat_s, ints, wt, cor_s, thick_s,
    a_src, a_dst, b_src, b_dst, y_dst, o_src, l_dst, r_dst, res,
    load_sem, small_sem, a_ss, a_rs, b_ss, b_rs, h_ss, h_rs, m_ss, m_rs, out_sem,
):
    lon, lat, dep = lax.axis_index("lon"), lax.axis_index("lat"), lax.axis_index("dep")
    ring_y, ring_z = lon % RING_Y, lon // RING_Y

    sources = (adj_t, merid, adj_v, adj_u, zonal)
    for i in (V, T, VV, UU, U):
        def load(z, c, i=i):
            pltpu.make_async_copy(
                sources[i].at[z], raw.at[i, pl.ds(HALO, OWN), z], load_sem.at[i]
            ).start()
            return c
        if i == V:
            smalls = [
                pltpu.make_async_copy(bottom, ints.at[0], small_sem.at[0]),
                pltpu.make_async_copy(atl, ints.at[1], small_sem.at[1]),
                pltpu.make_async_copy(weight_t, wt.at[0], small_sem.at[2]),
                pltpu.make_async_copy(target_t, wt.at[1], small_sem.at[3]),
                pltpu.make_async_copy(cor, cor_s, small_sem.at[4]),
                pltpu.make_async_copy(thick, thick_s, small_sem.at[5]),
            ]
            for copy in smalls:
                copy.start()
        lax.fori_loop(0, OWN, load, 0)

    def wait_load(i):
        pltpu.make_async_copy(
            sources[i], raw.at[i, pl.ds(HALO, OWN)], load_sem.at[i]
        ).wait()

    def wrap(i, n):
        return lax.rem(i + n, n)

    def ring_y_peer(k):
        return ring_z * RING_Y + lax.rem(ring_y + k, RING_Y)

    right, left = wrap(lon + 1, NLON), wrap(lon - 1, NLON)
    above, below = wrap(lat - 1, NLAT), wrap(lat + 1, NLAT)
    first_stage = []
    for slab, to_lat in ((0, lat), (1, below), (2, above)):
        for k in range(RING_Y):
            for d in range(NDEP):
                if slab == 0 and k == 0 and d == 0:
                    continue
                to_dep = dep if d == 0 else 1 - dep
                first_stage.append((slab, 2 * k + d, d, (ring_y_peer(k), to_lat, to_dep)))
    second_stage = [
        (k, (lax.rem(lon + RING_Y * k, NLON), lat, dep)) for k in range(1, RING_Z)
    ]
    around = [
        (right, lat, dep), (left, lat, dep),
        (right, above, dep), (left, above, dep), (right, below, dep), (left, below, dep),
    ]
    barrier = pltpu.get_barrier_semaphore()
    greeted = [p[3] for p in first_stage] + [p[1] for p in second_stage] + around
    for peer in greeted:
        pl.semaphore_signal(barrier, inc=1, device_id=peer, device_id_type=MESH)

    lane, sub = lanes(), sublanes()
    for copy in smalls:
        copy.wait()
    for y in range(0, OWN, 8):
        flat[0, pl.ds(HALO + y, 8)] = ints[0, pl.ds(y, 8)].astype(F32)
        flat[1, pl.ds(HALO + y, 8)] = ints[1, pl.ds(y, 8)].astype(F32)
        turning = jnp.zeros((8, 128), F32)
        for r in range(8):
            turning = jnp.where(sub == r, cor_s[y + r], turning)
        flat[2, pl.ds(HALO + y, 8)] = turning
    thickness = jnp.zeros((8, 128), F32)
    for z in range(OWN):
        here = jnp.logical_and(sub == z % 8, lane // 32 == z // 8)
        thickness = jnp.where(here, thick_s[z], thickness)

    depth_main = [(dep * OWN + 8 * g + sub).astype(F32) for g in range(4)]
    depth_strip = (dep * OWN + 8 * (lane // 32) + sub).astype(F32)

    def row(ref, i, y):
        return jnp.broadcast_to(ref[i, pl.ds(y, 1), :], (8, 128))

    wait_load(V)

    def basin_flow(i):
        g, y = i // OWN, HALO + i % OWN
        inside = depth_main[g] < row(flat, 0, y)
        return jnp.where(inside, raw[V, y, pl.ds(8 * g, 8), :], 0.0) * row(flat, 1, y)

    level_sum = reduce_lanes(basin_flow) * thickness

    def packed(i):
        filled = jnp.concatenate([wt[i], jnp.zeros((32, 64), F32)], axis=1)
        filled = jnp.concatenate([filled, jnp.zeros((96, 128), F32)], axis=0)
        turned = filled.T
        halves = []
        for half in range(2):
            tile = turned[32 * half:32 * half + 8]
            for g in range(1, 4):
                start = 32 * half + 8 * g
                tile = jnp.where(lane // 32 == g, lroll(turned[start:start + 8], 32 * g), tile)
            halves.append(tile)
        lower = dep == 1
        return jnp.where(lower, halves[1], halves[0]), jnp.where(lower, halves[0], halves[1])

    w_own, w_other = packed(0)
    g_own, g_other = packed(1)
    deeper, whole = suffix_tile(level_sum)
    is_low = jnp.where(dep == 1, 1.0, 0.0)
    mis_own = w_own * (deeper * (1.0 / 512.0) - g_own * (1.0 / 64.0))
    mis_other = w_other * (whole * is_low * (1.0 / 512.0) - g_other * (1.0 / 64.0))
    up_own, tot_own = prefix_tile(mis_own)
    up_other, tot_other = prefix_tile(mis_other)
    a_src[0] = up_own + is_low * tot_other
    a_src[1] = up_other + (1.0 - is_low) * tot_own

    pl.semaphore_wait(barrier, len(greeted))

    def send(src, dst, ss, rs, peer):
        copy = pltpu.make_async_remote_copy(
            src_ref=src, dst_ref=dst, send_sem=ss, recv_sem=rs,
            device_id=peer, device_id_type=MESH,
        )
        copy.start()
        return copy

    a_copies = [
        send(a_src.at[d], a_dst.at[slab, slot], a_ss.at[8 * slab + slot], a_rs.at[8 * slab + slot], peer)
        for slab, slot, d, peer in first_stage
    ]

    h_copies = []

    def halo_send(src, dst, peer):
        n = len(h_copies)
        h_copies.append(send(src, dst, h_ss.at[n], h_rs.at[n], peer))

    low, high = pl.ds(HALO, HALO), pl.ds(OWN, HALO)
    top, end = pl.ds(0, HALO), pl.ds(HALO + OWN, HALO)
    halo_send(flat.at[:, low], flat.at[:, end], (lon, above, dep))
    halo_send(flat.at[:, high], flat.at[:, top], (lon, below, dep))
    wait_load(T)
    wait_load(VV)
    wait_load(UU)
    wait_load(U)
    four_raw = pl.ds(0, 4)
    halo_send(raw.at[four_raw, low], raw.at[four_raw, end], (lon, above, dep))
    halo_send(raw.at[four_raw, high], raw.at[four_raw, top], (lon, below, dep))
    halo_send(raw.at[U, pl.ds(HALO, 6)], raw.at[U, pl.ds(HALO + OWN, 6)], (lon, above, dep))
    halo_send(raw.at[U, pl.ds(OWN + 2, 6)], raw.at[U, pl.ds(2, 6)], (lon, below, dep))

    for i in range(2):
        for y in range(0, OWN, 8):
            tile = flat[i, pl.ds(HALO + y, 8), :]
            flat_own[i, pl.ds(y, 8), :] = pack([tile] * 4)

    def pack_row(y):
        return [
            (strips_own, (i, y), pack([raw[i, HALO + y, pl.ds(8 * g, 8), :] for g in range(4)]))
            for i in range(5)
        ]

    by_rows(0, OWN, 4, pack_row)

    def strip_sends(put, src, dst_l, dst_r, own_lead):
        body, first, last = pl.ds(HALO, OWN), pl.ds(0, HALO), pl.ds(OWN - HALO, HALO)
        sl = (slice(None),) if own_lead else ()
        put(src, dst_l.at[sl + (body,)], (right, lat, dep))
        put(src, dst_r.at[sl + (body,)], (left, lat, dep))
        put(src.at[sl + (first,)], dst_l.at[sl + (end,)], (right, above, dep))
        put(src.at[sl + (first,)], dst_r.at[sl + (end,)], (left, above, dep))
        put(src.at[sl + (last,)], dst_l.at[sl + (top,)], (right, below, dep))
        put(src.at[sl + (last,)], dst_r.at[sl + (top,)], (left, below, dep))

    strip_sends(halo_send, flat_own, flat_l, flat_r, True)
    strip_sends(halo_send, strips_own, strips_l, strips_r, True)

    for copy in a_copies:
        copy.wait()
    a_dst[0, 0] = a_src[0]
    sums = []
    for slab in range(3):
        total = a_dst[slab, 0]
        for k in range(1, 8):
            total = total + a_dst[slab, k]
        sums.append(total)
    b_src[0] = sums[0]
    b_src[1] = jnp.where(lane % 32 >= 16, sums[1], sums[2])
    b_copies = [
        send(b_src, b_dst.at[k], b_ss.at[k], b_rs.at[k], peer) for k, peer in second_stage
    ]

    def prepare_row(y):
        deep = row(flat, 0, y)
        stores = []
        for g in range(4):
            at = pl.ds(8 * g, 8)
            inside = depth_main[g] < deep
            stores += [
                (mask, (y, at), jnp.where(inside, 1.0 / 12.0, 0.0)),
                (tr, (0, y, at), jnp.where(inside, raw[T, y, at, :], 0.0)),
                (uu, (y, at), jnp.where(inside, 3.0 * raw[UU, y, at, :], 0.0)),
            ]
        return stores

    by_rows(HALO, HALO + OWN, 4, prepare_row)

    for copy in h_copies:
        copy.wait()
    has_above = jnp.where(lat > 0, 1.0, 0.0)
    has_below = jnp.where(lat < NLAT - 1, 1.0, 0.0)
    flat[0, top] = flat[0, top] * has_above
    flat[0, end] = flat[0, end] * has_below
    by_rows(0, HALO, 4, prepare_row)
    by_rows(HALO + OWN, ROWS, 4, prepare_row)
    for y in range(0, ROWS, 8):
        at = pl.ds(y, 8)
        turning = flat[2, at]
        real, imag = jnp.ones((8, 128), F32), jnp.zeros((8, 128), F32)
        for k in range(9):
            coef[2 * k, at] = real
            coef[2 * k + 1, at] = imag
            real, imag = real - turning * imag, imag + turning * real
    for i in range(2):
        for y in range(0, ROWS, 8):
            at = pl.ds(y, 8)
            own = pack([flat[i, at, :]] * 4)
            flat_s[i, at, :] = merge(own, flat_l[i, at, :], flat_r[i, at, :])
    flat_s[0, top] = flat_s[0, top] * has_above
    flat_s[0, end] = flat_s[0, end] * has_below

    def strip_row(y, own):
        inside = depth_strip < row(flat_s, 0, y)
        stores = [(s_mask, y, jnp.where(inside, 1.0 / 12.0, 0.0))]
        for i in range(5):
            tile = merge(own(i), strips_l[i, y], strips_r[i, y])
            if i == T:
                stores.append((s_tr, (0, y), jnp.where(inside, tile, 0.0)))
                continue
            if i == UU:
                tile = jnp.where(inside, 3.0 * tile, 0.0)
            stores.append((s_raw, (i, y), tile))
        return stores

    by_rows(HALO, HALO + OWN, 4, lambda y: strip_row(y, lambda i: strips_own[i, y - HALO]))
    raw[U, pl.ds(0, 2)] = jnp.zeros((2, 32, 128), F32)
    raw[U, pl.ds(ROWS - 2, 2)] = jnp.zeros((2, 32, 128), F32)

    def strip_outer(y):
        return strip_row(
            y, lambda i: pack([raw[i, y, pl.ds(8 * g, 8), :] for g in range(4)])
        )

    by_rows(0, HALO, 4, strip_outer)
    by_rows(HALO + OWN, ROWS, 4, strip_outer)

    for copy in b_copies:
        copy.wait()
    ups = []
    for i in range(2):
        total = b_src[i]
        for k in range(1, RING_Z):
            total = total + b_dst[k, i]
        ups.append(total * thickness * 4.5)

    def gradient(y, up, offset):
        moved = pltpu.roll(up, lax.rem(256 + offset - y, 128), 1)
        spreads = [jnp.broadcast_to(moved[:, 32 * g:32 * g + 1], (8, 128)) for g in range(4)]
        basin = row(flat, 1, y)
        stores = []
        for g in range(4):
            at = pl.ds(8 * g, 8)
            value = mask[y, at, :] * (36.0 * raw[VV, y, at, :] + basin * spreads[g])
            stores.append((vv, (y, at), value))
        joined = spreads[0]
        for g in range(1, 4):
            joined = jnp.where(lane // 32 == g, spreads[g], joined)
        value = s_mask[y] * (36.0 * s_raw[VV, y] + row(flat_s, 1, y) * joined)
        stores.append((s_raw, (VV, y), value))
        return stores

    by_rows(HALO, HALO + OWN, 4, lambda y: gradient(y, ups[0], HALO))
    by_rows(0, HALO, 4, lambda y: gradient(y, ups[1], HALO - OWN))
    by_rows(HALO + OWN, ROWS, 4, lambda y: gradient(y, ups[1], HALO + OWN))

    edge = jnp.logical_or(lane < 2, lane >= 126)

    def column(k, first, last, get, emit):
        rows = range(first, ROWS - first)
        flux, held, us, vs = {}, {}, {}, {}

        def reach(y):
            held[y] = get("t", y)
            flux[y] = get("V", y) * held[y]

        def turn(y):
            u_0, v_0 = get("u", y), get("v", y)
            if k == 0:
                us[y], vs[y] = u_0, v_0
            else:
                real, imag = row(coef, 2 * k, y), row(coef, 2 * k + 1, y)
                us[y], vs[y] = real * u_0 - imag * v_0, real * v_0 + imag * u_0

        for y in range(first - 2, first + 2):
            reach(y)
        for y in (first - 1, first):
            turn(y)
        for y in rows:
            reach(y + 2)
            turn(y + 1)
            q_x = get("U", y) * held[y]
            a_x = 8.0 * q_x + us[y]
            z_x = (lroll(a_x, -1) - lroll(a_x, 1)) - (lroll(q_x, -2) - lroll(q_x, 2))
            z_y = 8.0 * (flux[y + 1] - flux[y - 1]) + (vs[y + 1] - vs[y - 1])
            z_y = z_y - (flux[y + 2] - flux[y - 2])
            scale = (1.0 / 12.0) if last else get("m", y)
            emit(y, held[y] + scale * (z_x + z_y))

    def step(k, first, last=False):
        now, new = k % 2, 1 - k % 2

        def strip_get(what, y):
            return {
                "t": lambda: s_tr[now, y], "u": lambda: s_raw[UU, y], "v": lambda: s_raw[VV, y],
                "m": lambda: s_mask[y], "U": lambda: s_raw[U, y], "V": lambda: s_raw[V, y],
            }[what]()

        def strip_emit(y, value):
            s_tr[new, y] = value
            s_edge[y] = spread(value)

        column(k, first, last, strip_get, strip_emit)

        def group(g, c):
            at = pl.ds(pl.multiple_of(8 * g, 8), 8)

            def get(what, y):
                return {
                    "t": lambda: tr[now, y, at, :], "u": lambda: uu[y, at, :],
                    "v": lambda: vv[y, at, :], "m": lambda: mask[y, at, :],
                    "U": lambda: raw[U, y, at, :], "V": lambda: raw[V, y, at, :],
                }[what]()

            def emit(y, value):
                fixed = pltpu.roll(s_edge[y], lax.rem(128 - 32 * g, 128), 1)
                tr[new, y, at, :] = jnp.where(edge, fixed, value)

            column(k, first, last, get, emit)
            return c

        lax.fori_loop(0, 4, group, 0)

    def refresh(y):
        own = pack([tr[0, y, pl.ds(8 * g, 8), :] for g in range(4)])
        place = lane % 32
        keep = jnp.logical_or(place < 8, place >= 24)
        return [(s_tr, (0, y), jnp.where(keep, s_tr[0, y], own))]

    def four(k, last=False):
        step(k, 2)
        step(k + 1, 4)
        by_rows(4, ROWS - 4, 8, refresh)
        step(k + 2, 6)
        step(k + 3, 8, last)

    four(0)

    m_copies = []

    def mid_send(src, dst, peer):
        n = len(m_copies)
        m_copies.append(send(src, dst, m_ss.at[n], m_rs.at[n], peer))

    mid_send(tr.at[0, low], y_dst.at[1], (lon, above, dep))
    mid_send(tr.at[0, high], y_dst.at[0], (lon, below, dep))

    def pack_tracer(y):
        return [(o_src, y, pack([tr[0, HALO + y, pl.ds(8 * g, 8), :] for g in range(4)]))]

    by_rows(0, OWN, 8, pack_tracer)
    strip_sends(mid_send, o_src, l_dst, r_dst, False)

    def turned(y):
        stores = []
        real, imag = row(coef, 16, y) * (1.0 / 3.0), row(coef, 17, y) * (1.0 / 3.0)
        for g in range(4):
            at = pl.ds(8 * g, 8)
            u_0, v_0 = uu[y, at, :], vv[y, at, :]
            stores.append((res, (0, y - HALO, at), real * u_0 - imag * v_0))
            stores.append((res, (1, y - HALO, at), real * v_0 + imag * u_0))
        return stores

    by_rows(HALO, HALO + OWN, 4, turned)

    def store_out(n, held, out):
        def store(z, c):
            pltpu.make_async_copy(held.at[:, z], out.at[z], out_sem.at[n]).start()
            return c
        lax.fori_loop(0, OWN, store, 0)

    store_out(0, res.at[0], out_u)
    store_out(1, res.at[1], out_v)

    for copy in m_copies:
        copy.wait()

    def halo_row(y):
        stores = []
        for n, at, valid in ((0, y, has_above), (1, HALO + OWN + y, has_below)):
            tiles = [y_dst[n, y, pl.ds(8 * g, 8), :] * valid for g in range(4)]
            stores += [(tr, (0, at, pl.ds(8 * g, 8)), tiles[g]) for g in range(4)]
            stores.append((s_tr, (0, at), merge(pack(tiles), l_dst[at] * valid, r_dst[at] * valid)))
        return stores

    by_rows(0, HALO, 4, halo_row)
    by_rows(
        HALO, HALO + OWN, 8,
        lambda y: [(s_tr, (0, y), merge(o_src[y - HALO], l_dst[y], r_dst[y]))],
    )
    four(4, True)

    result = tr.at[0, pl.ds(HALO, OWN)]
    store_out(2, result, out_t)
    for n, (held, out) in enumerate(((res.at[0], out_u), (res.at[1], out_v), (result, out_t))):
        pltpu.make_async_copy(held, out, out_sem.at[n]).wait()


def per_device(*args):
    args = args[:7] + (args[7].T, args[8].T) + args[9:]
    block = jax.ShapeDtypeStruct((32, 32, 128), F32)
    main = pltpu.VMEM((ROWS, 32, 128), F32)
    strip = pltpu.VMEM((ROWS, 8, 128), F32)
    dma = pltpu.SemaphoreType.DMA
    return pl.pallas_call(
        kernel,
        out_shape=(block,) * 3,
        in_specs=[pl.BlockSpec(memory_space=pltpu.HBM)] * 11,
        out_specs=(pl.BlockSpec(memory_space=pltpu.HBM),) * 3,
        scratch_shapes=[
            pltpu.VMEM((5, ROWS, 32, 128), F32),
            pltpu.VMEM((2, ROWS, 32, 128), F32),
            main, main, main,
            pltpu.VMEM((5, OWN, 8, 128), F32),
            pltpu.VMEM((5, ROWS, 8, 128), F32),
            pltpu.VMEM((5, ROWS, 8, 128), F32),
            pltpu.VMEM((5, ROWS, 8, 128), F32),
            strip,
            pltpu.VMEM((2, ROWS, 8, 128), F32),
            strip,
            pltpu.VMEM((3, ROWS, 128), F32),
            pltpu.VMEM((18, ROWS, 128), F32),
            pltpu.VMEM((2, OWN, 128), F32),
            pltpu.VMEM((2, ROWS, 128), F32),
            pltpu.VMEM((2, ROWS, 128), F32),
            pltpu.VMEM((2, ROWS, 128), F32),
            pltpu.VMEM((2, OWN, 128), jnp.int32),
            pltpu.VMEM((2, 32, 64), F32),
            pltpu.SMEM((32,), F32),
            pltpu.SMEM((32,), F32),
            pltpu.VMEM((2, 8, 128), F32),
            pltpu.VMEM((3, 8, 8, 128), F32),
            pltpu.VMEM((2, 8, 128), F32),
            pltpu.VMEM((8, 2, 8, 128), F32),
            pltpu.VMEM((2, HALO, 32, 128), F32),
            pltpu.VMEM((OWN, 8, 128), F32),
            strip, strip,
            pltpu.VMEM((2, OWN, 32, 128), F32),
            dma((5,)), dma((6,)), dma((24,)), dma((24,)), dma((8,)), dma((8,)),
            dma((18,)), dma((18,)), dma((8,)), dma((8,)), dma((3,)),
        ],
        compiler_params=pltpu.CompilerParams(
            collective_id=0, has_side_effects=True, vmem_limit_bytes=60 * 1024 * 1024
        ),
        name="adjoint",
    )(*args)


def solution(mesh):
    block, level = P("dep", "lat", "lon"), P(None, "lat")
    in_specs = (block,) * 5 + (P("lat"), P("dep"), level, level) + (P("lat", "lon"),) * 2
    return jax.shard_map(
        per_device, mesh=mesh, in_specs=in_specs, out_specs=(block,) * 3, check_vma=False
    )
```

profile of v0, /device:TPU:2, one launch (start us, length us, event | category | flops | bytes accessed | tf_op | source)
XLA Modules:
  0.0 81.5 jit_solution(4445646959337958306)
XLA Ops:
  0.6 76.9 %adjoint.1 = (f32[32,32,128]{2,1,0:T(8,128)}, f32[32,32,128]{2,1,0:T(8,128)}, f32[32,32,128]{2,1,0:T(8,128)}) custom-call(f32[32,32,128]{2,1,0:T(8,128)} %adj_u.1, f32[32,32,128]{2,1,0:T(8,128)} %adj_v.1, f32[32,32,128]{2,1,0:T(8,128)} %adj_t.1, f32[32,32,128]{2,1,0:T(8,128)} %zonal.1, f32[32,32,128]{2,1,0:T(8,128)} %merid.1, f32[32]{0:T(128)} %cor.1, ...), custom_call_target="tpu_custom_call" | custom-call | tf_op jit(solution)/shard_map/adjoint/pallas_call | solution.py:543
  77.6 0.0 copy-start.1
  77.6 1.9 %copy.17 = f32[32,32,128]{2,1,0:T(8,128)} copy(f32[32,32,128]{2,1,0:T(8,128)} %get-tuple-element.6) | data formatting | bytes 1048576
  79.5 0.0 copy-done.1
  79.5 0.0 copy-start
  79.5 0.8 copy.18
  80.3 0.4 copy-done
  80.7 0.8 copy.19
Async XLA Ops:
  77.6 1.9 %copy-start.1 = (f32[32,32,128]{2,1,0:T(8,128)S(1)}, f32[32,32,128]{2,1,0:T(8,128)}, u32[]{:S(2)}) copy-start(f32[32,32,128]{2,1,0:T(8,128)} %get-tuple-element.7) | copy-start | bytes 1572868
  79.5 1.2 %copy-start = (f32[32,32,128]{2,1,0:T(8,128)S(1)}, f32[32,32,128]{2,1,0:T(8,128)}, u32[]{:S(2)}) copy-start(f32[32,32,128]{2,1,0:T(8,128)} %get-tuple-element.8) | copy-start | bytes 1572868
where the time goes:
time: 81.7 us; the launch traced here: 81.5 us
  Pallas kernels  76.9 us (94%)
  local copies, waits for them, and re-layouts  3.95 us (5%)
    pallas_call x1, Pallas kernels, per_device(): pl.pallas_call(kernel, out_shape=(block,) * 3, in_specs=[pl.BlockSpec(mem...  76.9 us
    unnamed x7, local copies, waits for them, and re-layouts  3.95 us

commit v1 on v0

--- a/solution.py
+++ b/solution.py
@@ -7,6 +7,7 @@
 
 MESH = pl.DeviceIdType.MESH
 F32 = jnp.float32
+BF16 = jnp.bfloat16
 HALO = 8
 OWN = 32
 ROWS = OWN + 2 * HALO
@@ -40,15 +41,43 @@
     return jnp.where(lanes() % 32 < 16, lroll(joined, 8), lroll(joined, 24))
 
 
-def merge(own, left, right):
+def merge(own, left, right, slot=2, other=1):
     place = lanes() % 32
     return jnp.where(
-        place < 8, lroll(left, -16), jnp.where(place >= 24, lroll(right, 16), own)
+        place < 8,
+        lroll(left, -8 * slot),
+        jnp.where(place >= 24, lroll(right, 24 - 8 * other), own),
     )
 
 
-def spread(strip):
-    return jnp.where(lanes() % 32 < 16, lroll(strip, -8), lroll(strip, -24))
+def pack_four(strips):
+    at = lanes() // 8 % 4
+    both = []
+    for base in (16, 8):
+        joined = lroll(strips[0], -base)
+        for j in range(1, 4):
+            joined = jnp.where(at == j, lroll(strips[j], 8 * j - base), joined)
+        both.append(joined)
+    return both
+
+
+def slope_matrix(kind, group):
+    i = lax.broadcasted_iota(jnp.int32, (128, 128), 0)
+    j = lax.broadcasted_iota(jnp.int32, (128, 128), 1)
+    if group is not None:
+        place = i % 32
+        halo = jnp.logical_or(place < 8, place >= 24)
+        here = jnp.logical_and(halo, i // 32 == group)
+        i = jnp.where(here, jnp.where(place < 8, place - 8, place + 104), 1000)
+    apart = i - j
+    near, far = (8.0, 1.0) if kind == 0 else (1.0, 0.0)
+    out = jnp.where(apart == 1, near, jnp.where(apart == -1, -near, 0.0))
+    return out + jnp.where(apart == 2, -far, jnp.where(apart == -2, far, 0.0))
+
+
+def split(x):
+    high = x.astype(BF16)
+    return jnp.concatenate([high, (x - high.astype(F32)).astype(BF16)], axis=1)
 
 
 def suffix_tile(x):
@@ -107,9 +136,10 @@
 def kernel(
     adj_u, adj_v, adj_t, zonal, merid, cor, thick, weight_t, target_t, atl, bottom,
     out_u, out_v, out_t,
-    raw, tr, uu, vv, mask, strips_own, strips_l, strips_r, s_raw, s_mask, s_tr, s_edge,
+    raw, tr, uu, vv, mask, strips_own, strips_send, strips_l, strips_r, s_raw, s_mask, s_tr,
+    zx, corr, xu, xv, xb, s_xu, s_xv, s_xb, main_mat, strip_mat,
     flat, coef, flat_own, flat_l, flat_r, flat_s, ints, wt, cor_s, thick_s,
-    a_src, a_dst, b_src, b_dst, y_dst, o_src, l_dst, r_dst, res,
+    a_src, a_dst, b_src, b_dst, y_src, y_dst, o_src, o_send, l_dst, r_dst, res,
     load_sem, small_sem, a_ss, a_rs, b_ss, b_rs, h_ss, h_rs, m_ss, m_rs, out_sem,
 ):
     lon, lat, dep = lax.axis_index("lon"), lax.axis_index("lat"), lax.axis_index("dep")
@@ -183,6 +213,14 @@
         here = jnp.logical_and(sub == z % 8, lane // 32 == z // 8)
         thickness = jnp.where(here, thick_s[z], thickness)
 
+    for kind in range(2):
+        for n in range(5):
+            mat = slope_matrix(kind, None if n == 0 else n - 1).astype(BF16)
+            for half in range(2):
+                strip_mat[kind, pl.ds(128 * half, 128), pl.ds(128 * n, 128)] = mat
+                if n == 0:
+                    main_mat[kind, pl.ds(128 * half, 128), :] = mat
+
     depth_main = [(dep * OWN + 8 * g + sub).astype(F32) for g in range(4)]
     depth_strip = (dep * OWN + 8 * (lane // 32) + sub).astype(F32)
 
@@ -223,69 +261,128 @@
     a_src[0] = up_own + is_low * tot_other
     a_src[1] = up_other + (1.0 - is_low) * tot_own
 
+    def clear(rows, tiles, few, side, slab):
+        raw[:, rows] = jnp.zeros((5, HALO, 32, 128), F32)
+        flat[:, rows] = jnp.zeros((3, HALO, 128), F32)
+        a_dst[slab] = jnp.zeros((8, 8, 128), F32)
+        y_dst[side] = jnp.zeros((HALO, 32, 128), F32)
+        for ref in (strips_l, strips_r):
+            ref[tiles] = jnp.zeros((10, 8, 128), F32)
+        for ref in (flat_l, flat_r):
+            ref[:, rows] = jnp.zeros((2, HALO, 128), F32)
+        for ref in (l_dst, r_dst):
+            ref[few] = jnp.zeros((2, 8, 128), F32)
+
+    @pl.when(lat == 0)
+    def _():
+        clear(pl.ds(0, HALO), pl.ds(0, 10), pl.ds(0, 2), 0, 1)
+
+    @pl.when(lat == NLAT - 1)
+    def _():
+        clear(pl.ds(HALO + OWN, HALO), pl.ds(50, 10), pl.ds(10, 2), 1, 2)
+
     pl.semaphore_wait(barrier, len(greeted))
 
-    def send(src, dst, ss, rs, peer):
+    inner = {-1: lat > 0, 1: lat < NLAT - 1}
+
+    def when(condition, act):
+        if condition is None:
+            act()
+        else:
+            pl.when(condition)(act)
+
+    def send(src, dst, ss, rs, peer, toward=0):
         copy = pltpu.make_async_remote_copy(
             src_ref=src, dst_ref=dst, send_sem=ss, recv_sem=rs,
             device_id=peer, device_id_type=MESH,
         )
-        copy.start()
-        return copy
+        when(inner.get(toward), copy.start)
+        return copy, toward
+
+    def finish(copies):
+        for copy, toward in copies:
+            when(inner.get(-toward), copy.wait_recv)
+        for copy, toward in copies:
+            when(inner.get(toward), copy.wait_send)
 
     a_copies = [
-        send(a_src.at[d], a_dst.at[slab, slot], a_ss.at[8 * slab + slot], a_rs.at[8 * slab + slot], peer)
+        send(a_src.at[d], a_dst.at[slab, slot], a_ss.at[8 * slab + slot], a_rs.at[8 * slab + slot], peer, (0, 1, -1)[slab])
         for slab, slot, d, peer in first_stage
     ]
 
     h_copies = []
 
-    def halo_send(src, dst, peer):
+    def halo_send(src, dst, peer, toward=0):
         n = len(h_copies)
-        h_copies.append(send(src, dst, h_ss.at[n], h_rs.at[n], peer))
+        h_copies.append(send(src, dst, h_ss.at[n], h_rs.at[n], peer, toward))
 
     low, high = pl.ds(HALO, HALO), pl.ds(OWN, HALO)
     top, end = pl.ds(0, HALO), pl.ds(HALO + OWN, HALO)
-    halo_send(flat.at[:, low], flat.at[:, end], (lon, above, dep))
-    halo_send(flat.at[:, high], flat.at[:, top], (lon, below, dep))
-    wait_load(T)
-    wait_load(VV)
-    wait_load(UU)
-    wait_load(U)
-    four_raw = pl.ds(0, 4)
-    halo_send(raw.at[four_raw, low], raw.at[four_raw, end], (lon, above, dep))
-    halo_send(raw.at[four_raw, high], raw.at[four_raw, top], (lon, below, dep))
-    halo_send(raw.at[U, pl.ds(HALO, 6)], raw.at[U, pl.ds(HALO + OWN, 6)], (lon, above, dep))
-    halo_send(raw.at[U, pl.ds(OWN + 2, 6)], raw.at[U, pl.ds(2, 6)], (lon, below, dep))
-
+    halo_send(flat.at[:, low], flat.at[:, end], (lon, above, dep), -1)
+    halo_send(flat.at[:, high], flat.at[:, top], (lon, below, dep), 1)
     for i in range(2):
         for y in range(0, OWN, 8):
             tile = flat[i, pl.ds(HALO + y, 8), :]
             flat_own[i, pl.ds(y, 8), :] = pack([tile] * 4)
 
-    def pack_row(y):
-        return [
-            (strips_own, (i, y), pack([raw[i, HALO + y, pl.ds(8 * g, 8), :] for g in range(4)]))
-            for i in range(5)
-        ]
-
-    by_rows(0, OWN, 4, pack_row)
-
-    def strip_sends(put, src, dst_l, dst_r, own_lead):
+    def flat_sends():
         body, first, last = pl.ds(HALO, OWN), pl.ds(0, HALO), pl.ds(OWN - HALO, HALO)
-        sl = (slice(None),) if own_lead else ()
-        put(src, dst_l.at[sl + (body,)], (right, lat, dep))
-        put(src, dst_r.at[sl + (body,)], (left, lat, dep))
-        put(src.at[sl + (first,)], dst_l.at[sl + (end,)], (right, above, dep))
-        put(src.at[sl + (first,)], dst_r.at[sl + (end,)], (left, above, dep))
-        put(src.at[sl + (last,)], dst_l.at[sl + (top,)], (right, below, dep))
-        put(src.at[sl + (last,)], dst_r.at[sl + (top,)], (left, below, dep))
-
-    strip_sends(halo_send, flat_own, flat_l, flat_r, True)
-    strip_sends(halo_send, strips_own, strips_l, strips_r, True)
-
-    for copy in a_copies:
-        copy.wait()
+        for dst, to in ((flat_l, right), (flat_r, left)):
+            halo_send(flat_own, dst.at[:, body], (to, lat, dep))
+            halo_send(flat_own.at[:, first], dst.at[:, end], (to, above, dep), -1)
+            halo_send(flat_own.at[:, last], dst.at[:, top], (to, below, dep), 1)
+
+    flat_sends()
+    early_copies = list(h_copies)
+    for first, more, n in ((T, 2, 8), (VV, 2, 7), (U, 1, 6)):
+        pair = pl.ds(first, more)
+        for i in range(first, first + more):
+            if i != V:
+                wait_load(i)
+        halo_send(
+            raw.at[pair, pl.ds(HALO, n)], raw.at[pair, pl.ds(HALO + OWN, n)], (lon, above, dep),
+            -1,
+        )
+        halo_send(
+            raw.at[pair, pl.ds(HALO + OWN - n, n)], raw.at[pair, pl.ds(HALO - n, n)],
+            (lon, below, dep), 1,
+        )
+
+    def pack_block(n):
+        stores = []
+        own = {}
+        for r in range(4):
+            for i in range(5):
+                y = HALO + 4 * n + r
+                own[i, r] = pack([raw[i, y, pl.ds(8 * g, 8), :] for g in range(4)])
+                stores.append((strips_own, (i, 4 * n + r), own[i, r]))
+        for r in range(5):
+            tiles = [own[i, r] for i in range(4)] if r < 4 else [own[U, q] for q in range(4)]
+            to_right, to_left = pack_four(tiles)
+            stores.append((strips_send, (0, 5 * n + r), to_right))
+            stores.append((strips_send, (1, 5 * n + r), to_left))
+        return stores
+
+    by_rows(0, OWN // 4, 1, pack_block)
+
+    def strip_sends(put, src_r, src_l, dst_l, dst_r, edge):
+        body = src_r.shape[-3] if len(src_r.shape) == 3 else src_r.shape[-2]
+        sl = (slice(None),) * (0 if len(src_r.shape) == 3 else 1)
+        here, first, last = pl.ds(edge, body), pl.ds(0, edge), pl.ds(body - edge, edge)
+        after = pl.ds(body + edge, edge)
+        put(src_r, dst_l.at[sl + (here,)], (right, lat, dep))
+        put(src_l, dst_r.at[sl + (here,)], (left, lat, dep))
+        put(src_r.at[sl + (first,)], dst_l.at[sl + (after,)], (right, above, dep), -1)
+        put(src_l.at[sl + (first,)], dst_r.at[sl + (after,)], (left, above, dep), -1)
+        put(src_r.at[sl + (last,)], dst_l.at[sl + (first,)], (right, below, dep), 1)
+        put(src_l.at[sl + (last,)], dst_r.at[sl + (first,)], (left, below, dep), 1)
+
+    strips_from = len(h_copies)
+    strip_sends(halo_send, strips_send.at[0], strips_send.at[1], strips_l, strips_r, 10)
+    early_copies += h_copies[strips_from:strips_from + 2]
+    late_copies = h_copies[len(early_copies) - 2:strips_from] + h_copies[strips_from + 2:]
+
+    finish(a_copies)
     a_dst[0, 0] = a_src[0]
     sums = []
     for slab in range(3):
@@ -314,14 +411,11 @@
 
     by_rows(HALO, HALO + OWN, 4, prepare_row)
 
-    for copy in h_copies:
-        copy.wait()
+    finish(early_copies)
     has_above = jnp.where(lat > 0, 1.0, 0.0)
     has_below = jnp.where(lat < NLAT - 1, 1.0, 0.0)
     flat[0, top] = flat[0, top] * has_above
     flat[0, end] = flat[0, end] * has_below
-    by_rows(0, HALO, 4, prepare_row)
-    by_rows(HALO + OWN, ROWS, 4, prepare_row)
     for y in range(0, ROWS, 8):
         at = pl.ds(y, 8)
         turning = flat[2, at]
@@ -338,33 +432,66 @@
     flat_s[0, top] = flat_s[0, top] * has_above
     flat_s[0, end] = flat_s[0, end] * has_below
 
-    def strip_row(y, own):
-        inside = depth_strip < row(flat_s, 0, y)
-        stores = [(s_mask, y, jnp.where(inside, 1.0 / 12.0, 0.0))]
-        for i in range(5):
-            tile = merge(own(i), strips_l[i, y], strips_r[i, y])
-            if i == T:
-                stores.append((s_tr, (0, y), jnp.where(inside, tile, 0.0)))
-                continue
-            if i == UU:
-                tile = jnp.where(inside, 3.0 * tile, 0.0)
-            stores.append((s_raw, (i, y), tile))
+    def strip_block(n, own):
+        stores = []
+        for r in range(4):
+            y = 4 * n + r
+            inside = depth_strip < row(flat_s, 0, y)
+            stores.append((s_mask, y, jnp.where(inside, 1.0 / 12.0, 0.0)))
+            for i in range(5):
+                at, slot = (5 * n + r, i) if i < 4 else (5 * n + 4, r)
+                tile = merge(own(i, r), strips_l[at], strips_r[at], slot, slot)
+                if i == T:
+                    stores.append((s_tr, (0, y), jnp.where(inside, tile, 0.0)))
+                    continue
+                if i == UU:
+                    tile = jnp.where(inside, 3.0 * tile, 0.0)
+                stores.append((s_raw, (i, y), tile))
         return stores
 
-    by_rows(HALO, HALO + OWN, 4, lambda y: strip_row(y, lambda i: strips_own[i, y - HALO]))
-    raw[U, pl.ds(0, 2)] = jnp.zeros((2, 32, 128), F32)
-    raw[U, pl.ds(ROWS - 2, 2)] = jnp.zeros((2, 32, 128), F32)
-
-    def strip_outer(y):
-        return strip_row(
-            y, lambda i: pack([raw[i, y, pl.ds(8 * g, 8), :] for g in range(4)])
+    by_rows(
+        2, 10, 1, lambda n: strip_block(n, lambda i, r: strips_own[i, 4 * n + r - HALO])
+    )
+    def slope(kind, low, high, main, strip, main_out, strip_out, fold):
+        count = high - low
+        got = jnp.dot(
+            split(strip(pl.ds(low, count)).reshape(8 * count, 128)),
+            strip_mat[kind], preferred_element_type=F32,
         )
-
-    by_rows(0, HALO, 4, strip_outer)
-    by_rows(HALO + OWN, ROWS, 4, strip_outer)
-
-    for copy in b_copies:
-        copy.wait()
+        strip_out[pl.ds(low, count)] = got[:, :128].reshape(count, 8, 128)
+        edges = [
+            got[:, 128 * g + 128:128 * g + 256].reshape(count, 8, 128) for g in range(4)
+        ]
+        if not fold:
+            for g in range(4):
+                corr[g, pl.ds(low, count)] = edges[g]
+        parts = 4 if count > 8 else 1
+        part = count // parts
+        for n in range(parts):
+            at = pl.ds(low + part * n, part)
+            out = jnp.dot(
+                split(main(at).reshape(32 * part, 128)), main_mat[kind],
+                preferred_element_type=F32,
+            ).reshape(part, 32, 128)
+            if fold:
+                mine = [e[part * n:part * n + part] for e in edges]
+                out = out + jnp.concatenate(mine, axis=1)
+            main_out[at] = out
+
+    def fixed_slopes(low, high):
+        slope(1, low, high, lambda at: uu[at], lambda at: s_raw[UU, at], xu, s_xu, True)
+        slope(
+            1, low, high, lambda at: 36.0 * mask[at] * raw[VV, at],
+            lambda at: 36.0 * s_mask[at] * s_raw[VV, at], xv, s_xv, True,
+        )
+        slope(
+            1, low, high, lambda at: mask[at] * flat[1, at][:, None, :],
+            lambda at: s_mask[at] * flat_s[1, at][:, None, :], xb, s_xb, True,
+        )
+
+    fixed_slopes(HALO, HALO + OWN)
+
+    finish(b_copies)
     ups = []
     for i in range(2):
         total = b_src[i]
@@ -381,64 +508,69 @@
             at = pl.ds(8 * g, 8)
             value = mask[y, at, :] * (36.0 * raw[VV, y, at, :] + basin * spreads[g])
             stores.append((vv, (y, at), value))
+            stores.append((xv, (y, at), xv[y, at, :] + spreads[g] * xb[y, at, :]))
         joined = spreads[0]
         for g in range(1, 4):
             joined = jnp.where(lane // 32 == g, spreads[g], joined)
         value = s_mask[y] * (36.0 * s_raw[VV, y] + row(flat_s, 1, y) * joined)
         stores.append((s_raw, (VV, y), value))
+        stores.append((s_xv, y, s_xv[y] + joined * s_xb[y]))
         return stores
 
     by_rows(HALO, HALO + OWN, 4, lambda y: gradient(y, ups[0], HALO))
-    by_rows(0, HALO, 4, lambda y: gradient(y, ups[1], HALO - OWN))
-    by_rows(HALO + OWN, ROWS, 4, lambda y: gradient(y, ups[1], HALO + OWN))
-
-    edge = jnp.logical_or(lane < 2, lane >= 126)
-
-    def column(k, first, last, get, emit):
-        rows = range(first, ROWS - first)
-        flux, held, us, vs = {}, {}, {}, {}
+    def column(k, low, high, last, get, emit):
+        flux, held, vs = {}, {}, {}
 
         def reach(y):
             held[y] = get("t", y)
             flux[y] = get("V", y) * held[y]
 
         def turn(y):
-            u_0, v_0 = get("u", y), get("v", y)
             if k == 0:
-                us[y], vs[y] = u_0, v_0
+                vs[y] = get("v", y)
             else:
-                real, imag = row(coef, 2 * k, y), row(coef, 2 * k + 1, y)
-                us[y], vs[y] = real * u_0 - imag * v_0, real * v_0 + imag * u_0
-
-        for y in range(first - 2, first + 2):
+                vs[y] = row(coef, 2 * k, y) * get("v", y) + row(coef, 2 * k + 1, y) * get("u", y)
+
+        for y in range(low - 2, low + 2):
             reach(y)
-        for y in (first - 1, first):
+        for y in (low - 1, low):
             turn(y)
-        for y in rows:
+        for y in range(low, high):
             reach(y + 2)
             turn(y + 1)
-            q_x = get("U", y) * held[y]
-            a_x = 8.0 * q_x + us[y]
-            z_x = (lroll(a_x, -1) - lroll(a_x, 1)) - (lroll(q_x, -2) - lroll(q_x, 2))
+            z_x = get("zx", y)
+            if k == 0:
+                z_x = z_x + get("xu", y)
+            else:
+                z_x = z_x + (
+                    row(coef, 2 * k, y) * get("xu", y) - row(coef, 2 * k + 1, y) * get("xv", y)
+                )
             z_y = 8.0 * (flux[y + 1] - flux[y - 1]) + (vs[y + 1] - vs[y - 1])
             z_y = z_y - (flux[y + 2] - flux[y - 2])
             scale = (1.0 / 12.0) if last else get("m", y)
             emit(y, held[y] + scale * (z_x + z_y))
 
-    def step(k, first, last=False):
+    def step(k, ranges, last):
         now, new = k % 2, 1 - k % 2
+        for low, high in ranges:
+            slope(
+                0, low, high, lambda at: raw[U, at] * tr[now, at],
+                lambda at: s_raw[U, at] * s_tr[now, at], zx, corr.at[4], False,
+            )
 
         def strip_get(what, y):
             return {
                 "t": lambda: s_tr[now, y], "u": lambda: s_raw[UU, y], "v": lambda: s_raw[VV, y],
-                "m": lambda: s_mask[y], "U": lambda: s_raw[U, y], "V": lambda: s_raw[V, y],
+                "m": lambda: s_mask[y], "V": lambda: s_raw[V, y],
+                "zx": lambda: corr[4, y], "xu": lambda: s_xu[y], "xv": lambda: s_xv[y],
             }[what]()
 
         def strip_emit(y, value):
             s_tr[new, y] = value
-            s_edge[y] = spread(value)
-
-        column(k, first, last, strip_get, strip_emit)
+
+        if not last:
+            for low, high in ranges:
+                column(k, low, high, False, strip_get, strip_emit)
 
         def group(g, c):
             at = pl.ds(pl.multiple_of(8 * g, 8), 8)
@@ -447,47 +579,75 @@
                 return {
                     "t": lambda: tr[now, y, at, :], "u": lambda: uu[y, at, :],
                     "v": lambda: vv[y, at, :], "m": lambda: mask[y, at, :],
-                    "U": lambda: raw[U, y, at, :], "V": lambda: raw[V, y, at, :],
+                    "V": lambda: raw[V, y, at, :],
+                    "zx": lambda: zx[y, at, :] + corr[g, y],
+                    "xu": lambda: xu[y, at, :], "xv": lambda: xv[y, at, :],
                 }[what]()
 
             def emit(y, value):
-                fixed = pltpu.roll(s_edge[y], lax.rem(128 - 32 * g, 128), 1)
-                tr[new, y, at, :] = jnp.where(edge, fixed, value)
-
-            column(k, first, last, get, emit)
+                tr[new, y, at, :] = value
+
+            for low, high in ranges:
+                column(k, low, high, last, get, emit)
             return c
 
         lax.fori_loop(0, 4, group, 0)
 
-    def refresh(y):
-        own = pack([tr[0, y, pl.ds(8 * g, 8), :] for g in range(4)])
-        place = lane % 32
-        keep = jnp.logical_or(place < 8, place >= 24)
-        return [(s_tr, (0, y), jnp.where(keep, s_tr[0, y], own))]
-
-    def four(k, last=False):
-        step(k, 2)
-        step(k + 1, 4)
-        by_rows(4, ROWS - 4, 8, refresh)
-        step(k + 2, 6)
-        step(k + 3, 8, last)
-
-    four(0)
+    def inner_rows(k, last):
+        for n in range(1, 5):
+            step(k + n - 1, ((HALO + 2 * n, HALO + OWN - 2 * n),), last and n == 4)
+
+    def outer_rows(k, last):
+        for n in range(1, 5):
+            low, high = 2 * n, ROWS - 2 * n
+            step(k + n - 1, ((low, low + HALO), (high - HALO, high)), last and n == 4)
+
+    inner_rows(0, False)
+    finish(late_copies)
+    by_rows(0, HALO, 4, prepare_row)
+    by_rows(HALO + OWN, ROWS, 4, prepare_row)
+    for outer in (0, ROWS - 2):
+        raw[U, pl.ds(outer, 2)] = jnp.zeros((2, 32, 128), F32)
+    for outer in (0, ROWS - 1):
+        raw[pl.ds(2, 2), outer] = jnp.zeros((2, 32, 128), F32)
+
+    def strip_outer(n):
+        return strip_block(
+            n, lambda i, r: pack([raw[i, 4 * n + r, pl.ds(8 * g, 8), :] for g in range(4)])
+        )
+
+    by_rows(0, 2, 1, strip_outer)
+    by_rows(10, 12, 1, strip_outer)
+
+    fixed_slopes(2, HALO)
+    fixed_slopes(HALO + OWN, ROWS - 2)
+    by_rows(0, HALO, 4, lambda y: gradient(y, ups[1], HALO - OWN))
+    by_rows(HALO + OWN, ROWS, 4, lambda y: gradient(y, ups[1], HALO + OWN))
+    outer_rows(0, False)
 
     m_copies = []
 
-    def mid_send(src, dst, peer):
+    def mid_send(src, dst, peer, toward=0):
         n = len(m_copies)
-        m_copies.append(send(src, dst, m_ss.at[n], m_rs.at[n], peer))
-
-    mid_send(tr.at[0, low], y_dst.at[1], (lon, above, dep))
-    mid_send(tr.at[0, high], y_dst.at[0], (lon, below, dep))
-
-    def pack_tracer(y):
-        return [(o_src, y, pack([tr[0, HALO + y, pl.ds(8 * g, 8), :] for g in range(4)]))]
-
-    by_rows(0, OWN, 8, pack_tracer)
-    strip_sends(mid_send, o_src, l_dst, r_dst, False)
+        m_copies.append(send(src, dst, m_ss.at[n], m_rs.at[n], peer, toward))
+
+    y_src[0] = tr[0, low]
+    y_src[1] = tr[0, high]
+    mid_send(y_src.at[0], y_dst.at[1], (lon, above, dep), -1)
+    mid_send(y_src.at[1], y_dst.at[0], (lon, below, dep), 1)
+
+    def pack_tracer(n):
+        own = [
+            pack([tr[0, HALO + 4 * n + r, pl.ds(8 * g, 8), :] for g in range(4)])
+            for r in range(4)
+        ]
+        both = pack_four(own)
+        return [(o_src, 4 * n + r, own[r]) for r in range(4)] + [
+            (o_send, (i, n), both[i]) for i in range(2)
+        ]
+
+    by_rows(0, OWN // 4, 2, pack_tracer)
+    strip_sends(mid_send, o_send.at[0], o_send.at[1], l_dst, r_dst, 2)
 
     def turned(y):
         stores = []
@@ -510,23 +670,33 @@
     store_out(0, res.at[0], out_u)
     store_out(1, res.at[1], out_v)
 
-    for copy in m_copies:
-        copy.wait()
-
-    def halo_row(y):
+    finish(m_copies[2:4])
+
+    def own_block(n):
+        return [
+            (s_tr, (0, HALO + 4 * n + r), merge(o_src[4 * n + r], l_dst[2 + n], r_dst[2 + n], r, r))
+            for r in range(4)
+        ]
+
+    by_rows(0, OWN // 4, 2, own_block)
+    inner_rows(4, True)
+    finish(m_copies[:2] + m_copies[4:])
+
+    def halo_block(n):
         stores = []
-        for n, at, valid in ((0, y, has_above), (1, HALO + OWN + y, has_below)):
-            tiles = [y_dst[n, y, pl.ds(8 * g, 8), :] * valid for g in range(4)]
-            stores += [(tr, (0, at, pl.ds(8 * g, 8)), tiles[g]) for g in range(4)]
-            stores.append((s_tr, (0, at), merge(pack(tiles), l_dst[at] * valid, r_dst[at] * valid)))
+        for r in range(4):
+            for side, at, block, valid in (
+                (0, 4 * n + r, n, has_above),
+                (1, HALO + OWN + 4 * n + r, 10 + n, has_below),
+            ):
+                tiles = [y_dst[side, 4 * n + r, pl.ds(8 * g, 8), :] * valid for g in range(4)]
+                stores += [(tr, (0, at, pl.ds(8 * g, 8)), tiles[g]) for g in range(4)]
+                strip = merge(pack(tiles), l_dst[block] * valid, r_dst[block] * valid, r, r)
+                stores.append((s_tr, (0, at), strip))
         return stores
 
-    by_rows(0, HALO, 4, halo_row)
-    by_rows(
-        HALO, HALO + OWN, 8,
-        lambda y: [(s_tr, (0, y), merge(o_src[y - HALO], l_dst[y], r_dst[y]))],
-    )
-    four(4, True)
+    by_rows(0, 2, 1, halo_block)
+    outer_rows(4, True)
 
     result = tr.at[0, pl.ds(HALO, OWN)]
     store_out(2, result, out_t)
@@ -550,12 +720,17 @@
             pltpu.VMEM((2, ROWS, 32, 128), F32),
             main, main, main,
             pltpu.VMEM((5, OWN, 8, 128), F32),
-            pltpu.VMEM((5, ROWS, 8, 128), F32),
-            pltpu.VMEM((5, ROWS, 8, 128), F32),
+            pltpu.VMEM((2, 40, 8, 128), F32),
+            pltpu.VMEM((60, 8, 128), F32),
+            pltpu.VMEM((60, 8, 128), F32),
             pltpu.VMEM((5, ROWS, 8, 128), F32),
             strip,
             pltpu.VMEM((2, ROWS, 8, 128), F32),
-            strip,
+            main,
+            pltpu.VMEM((5, ROWS, 8, 128), F32),
+            main, main, main, strip, strip, strip,
+            pltpu.VMEM((2, 256, 128), BF16),
+            pltpu.VMEM((2, 256, 640), BF16),
             pltpu.VMEM((3, ROWS, 128), F32),
             pltpu.VMEM((18, ROWS, 128), F32),
             pltpu.VMEM((2, OWN, 128), F32),
@@ -571,11 +746,14 @@
             pltpu.VMEM((2, 8, 128), F32),
             pltpu.VMEM((8, 2, 8, 128), F32),
             pltpu.VMEM((2, HALO, 32, 128), F32),
+            pltpu.VMEM((2, HALO, 32, 128), F32),
             pltpu.VMEM((OWN, 8, 128), F32),
-            strip, strip,
+            pltpu.VMEM((2, 8, 8, 128), F32),
+            pltpu.VMEM((12, 8, 128), F32),
+            pltpu.VMEM((12, 8, 128), F32),
             pltpu.VMEM((2, OWN, 32, 128), F32),
             dma((5,)), dma((6,)), dma((24,)), dma((24,)), dma((8,)), dma((8,)),
-            dma((18,)), dma((18,)), dma((8,)), dma((8,)), dma((3,)),
+            dma((20,)), dma((20,)), dma((8,)), dma((8,)), dma((3,)),
         ],
         compiler_params=pltpu.CompilerParams(
             collective_id=0, has_side_effects=True, vmem_limit_bytes=60 * 1024 * 1024

time: 81.7 us -> 52.4 us (0.64)
  Pallas kernels: 76.9 us -> 47.7 us
    pallas_call x1, Pallas kernels: 76.9 us -> 47.7 us  [per_device(): pl.pallas_call(kernel, out_shape=(block,) * 3, in_specs=[pl.BlockSpec(mem...]
where the time goes in v1:
time: 52.4 us; the launch traced here: 52.3 us
  Pallas kernels  47.7 us (91%)
  local copies, waits for them, and re-layouts  3.95 us (8%)
  between operations  0.65 us (1%)
    pallas_call x1, Pallas kernels, per_device(): pl.pallas_call(kernel, out_shape=(block,) * 3, in_specs=[pl.BlockSpec(mem...  47.7 us
    unnamed x7, local copies, waits for them, and re-layouts  3.95 us

profile of v1, /device:TPU:2, one launch (start us, length us, event | category | flops | bytes accessed | tf_op | source)
XLA Modules:
  0.0 52.3 jit_solution(16653619800464645466)
XLA Ops:
  0.6 47.7 %adjoint.1 = (f32[32,32,128]{2,1,0:T(8,128)}, f32[32,32,128]{2,1,0:T(8,128)}, f32[32,32,128]{2,1,0:T(8,128)}) custom-call(f32[32,32,128]{2,1,0:T(8,128)} %adj_u.1, f32[32,32,128]{2,1,0:T(8,128)} %adj_v.1, f32[32,32,128]{2,1,0:T(8,128)} %adj_t.1, f32[32,32,128]{2,1,0:T(8,128)} %zonal.1, f32[32,32,128]{2,1,0:T(8,128)} %merid.1, f32[32]{0:T(128)} %cor.1, ...), custom_call_target="tpu_custom_call" | custom-call | tf_op jit(solution)/shard_map/adjoint/pallas_call | solution.py:713
  48.3 0.0 copy-start.1
  48.3 1.9 %copy.17 = f32[32,32,128]{2,1,0:T(8,128)} copy(f32[32,32,128]{2,1,0:T(8,128)} %get-tuple-element.6) | data formatting | bytes 1048576
  50.2 0.0 copy-done.1
  50.2 0.0 copy-start
  50.2 0.8 %copy.18 = f32[32,32,128]{2,1,0:T(8,128)} copy(f32[32,32,128]{2,1,0:T(8,128)S(1)} %copy-done.1) | data formatting | bytes 1048576
  51.0 0.4 copy-done
  51.5 0.8 %copy.19 = f32[32,32,128]{2,1,0:T(8,128)} copy(f32[32,32,128]{2,1,0:T(8,128)S(1)} %copy-done) | data formatting | bytes 1048576
Async XLA Ops:
  48.3 1.9 %copy-start.1 = (f32[32,32,128]{2,1,0:T(8,128)S(1)}, f32[32,32,128]{2,1,0:T(8,128)}, u32[]{:S(2)}) copy-start(f32[32,32,128]{2,1,0:T(8,128)} %get-tuple-element.7) | copy-start | bytes 1572868
  50.2 1.2 %copy-start = (f32[32,32,128]{2,1,0:T(8,128)S(1)}, f32[32,32,128]{2,1,0:T(8,128)}, u32[]{:S(2)}) copy-start(f32[32,32,128]{2,1,0:T(8,128)} %get-tuple-element.8) | copy-start | bytes 1572868

commit v2 on v1

--- a/solution.py
+++ b/solution.py
@@ -139,8 +139,8 @@
     raw, tr, uu, vv, mask, strips_own, strips_send, strips_l, strips_r, s_raw, s_mask, s_tr,
     zx, corr, xu, xv, xb, s_xu, s_xv, s_xb, main_mat, strip_mat,
     flat, coef, flat_own, flat_l, flat_r, flat_s, ints, wt, cor_s, thick_s,
-    a_src, a_dst, b_src, b_dst, y_src, y_dst, o_src, o_send, l_dst, r_dst, res,
-    load_sem, small_sem, a_ss, a_rs, b_ss, b_rs, h_ss, h_rs, m_ss, m_rs, out_sem,
+    a_src, a_dst, b_src, b_dst, y_src, y_dst, o_src, o_send, l_dst, r_dst,
+    load_sem, small_sem, a_ss, a_rs, b_ss, b_rs, h_ss, h_rs, m_ss, m_rs,
 ):
     lon, lat, dep = lax.axis_index("lon"), lax.axis_index("lat"), lax.axis_index("dep")
     ring_y, ring_z = lon % RING_Y, lon // RING_Y
@@ -585,7 +585,10 @@
                 }[what]()
 
             def emit(y, value):
-                tr[new, y, at, :] = value
+                if last:
+                    out_t[y - HALO, at, :] = value
+                else:
+                    tr[new, y, at, :] = value
 
             for low, high in ranges:
                 column(k, low, high, last, get, emit)
@@ -655,20 +658,11 @@
         for g in range(4):
             at = pl.ds(8 * g, 8)
             u_0, v_0 = uu[y, at, :], vv[y, at, :]
-            stores.append((res, (0, y - HALO, at), real * u_0 - imag * v_0))
-            stores.append((res, (1, y - HALO, at), real * v_0 + imag * u_0))
+            stores.append((out_u, (y - HALO, at), real * u_0 - imag * v_0))
+            stores.append((out_v, (y - HALO, at), real * v_0 + imag * u_0))
         return stores
 
     by_rows(HALO, HALO + OWN, 4, turned)
-
-    def store_out(n, held, out):
-        def store(z, c):
-            pltpu.make_async_copy(held.at[:, z], out.at[z], out_sem.at[n]).start()
-            return c
-        lax.fori_loop(0, OWN, store, 0)
-
-    store_out(0, res.at[0], out_u)
-    store_out(1, res.at[1], out_v)
 
     finish(m_copies[2:4])
 
@@ -698,23 +692,29 @@
     by_rows(0, 2, 1, halo_block)
     outer_rows(4, True)
 
-    result = tr.at[0, pl.ds(HALO, OWN)]
-    store_out(2, result, out_t)
-    for n, (held, out) in enumerate(((res.at[0], out_u), (res.at[1], out_v), (result, out_t))):
-        pltpu.make_async_copy(held, out, out_sem.at[n]).wait()
+
+def store(*refs):
+    held, outs, sem = refs[:3], refs[3:6], refs[6]
+    for n in range(3):
+        def level(z, c, n=n):
+            pltpu.make_async_copy(held[n].at[:, z], outs[n].at[z], sem.at[n]).start()
+            return c
+        lax.fori_loop(0, OWN, level, 0)
+    for n in range(3):
+        pltpu.make_async_copy(held[n], outs[n], sem.at[n]).wait()
 
 
 def per_device(*args):
     args = args[:7] + (args[7].T, args[8].T) + args[9:]
-    block = jax.ShapeDtypeStruct((32, 32, 128), F32)
+    held = pltpu.VMEM((32, 32, 128), F32)
     main = pltpu.VMEM((ROWS, 32, 128), F32)
     strip = pltpu.VMEM((ROWS, 8, 128), F32)
     dma = pltpu.SemaphoreType.DMA
-    return pl.pallas_call(
+    results = pl.pallas_call(
         kernel,
-        out_shape=(block,) * 3,
+        out_shape=(held,) * 3,
         in_specs=[pl.BlockSpec(memory_space=pltpu.HBM)] * 11,
-        out_specs=(pl.BlockSpec(memory_space=pltpu.HBM),) * 3,
+        out_specs=(pl.BlockSpec(memory_space=pltpu.VMEM),) * 3,
         scratch_shapes=[
             pltpu.VMEM((5, ROWS, 32, 128), F32),
             pltpu.VMEM((2, ROWS, 32, 128), F32),
@@ -751,15 +751,23 @@
             pltpu.VMEM((2, 8, 8, 128), F32),
             pltpu.VMEM((12, 8, 128), F32),
             pltpu.VMEM((12, 8, 128), F32),
-            pltpu.VMEM((2, OWN, 32, 128), F32),
             dma((5,)), dma((6,)), dma((24,)), dma((24,)), dma((8,)), dma((8,)),
-            dma((20,)), dma((20,)), dma((8,)), dma((8,)), dma((3,)),
+            dma((20,)), dma((20,)), dma((8,)), dma((8,)),
         ],
         compiler_params=pltpu.CompilerParams(
             collective_id=0, has_side_effects=True, vmem_limit_bytes=60 * 1024 * 1024
         ),
         name="adjoint",
     )(*args)
+    return pl.pallas_call(
+        store,
+        out_shape=(jax.ShapeDtypeStruct((32, 32, 128), F32),) * 3,
+        in_specs=[pl.BlockSpec(memory_space=pltpu.VMEM)] * 3,
+        out_specs=(pl.BlockSpec(memory_space=pltpu.HBM),) * 3,
+        scratch_shapes=[dma((3,))],
+        compiler_params=pltpu.CompilerParams(vmem_limit_bytes=4 * 1024 * 1024),
+        name="store",
+    )(*results)
 
 
 def solution(mesh):

time: 52.4 us -> 48.9 us (0.933)
  local copies, waits for them, and re-layouts: 3.95 us -> 0 us
    unnamed x7 -> x0, local copies, waits for them, and re-layouts: 3.95 us -> none
    pallas_call x1 -> x2, Pallas kernels: 47.7 us -> 48.2 us  [the longest x1 46.8 us: per_device(): pl.pallas_call(kernel, out_shape=(held,) * 3, in_specs=[pl.BlockSpec(memo...]
where the time goes in v2:
time: 48.9 us; the launch traced here: 48.8 us
  Pallas kernels  48.2 us (99%)
  between operations  0.64 us (1%)
    pallas_call x1, Pallas kernels, per_device(): pl.pallas_call(kernel, out_shape=(held,) * 3, in_specs=[pl.BlockSpec(memo...  46.8 us
    pallas_call x1, Pallas kernels, per_device(): pl.pallas_call(store, out_shape=(jax.ShapeDtypeStruct((32, 32, 128), F32)...  1.36 us

profile of v2, /device:TPU:2, one launch (start us, length us, event | category | flops | bytes accessed | tf_op | source)
XLA Modules:
  0.0 48.8 jit_solution(5490031282295121240)
XLA Ops:
  0.6 46.8 %adjoint.1 = (f32[32,32,128]{2,1,0:T(8,128)S(1)}, f32[32,32,128]{2,1,0:T(8,128)S(1)}, f32[32,32,128]{2,1,0:T(8,128)S(1)}) custom-call(f32[32,32,128]{2,1,0:T(8,128)} %adj_u.1, f32[32,32,128]{2,1,0:T(8,128)} %adj_v.1, f32[32,32,128]{2,1,0:T(8,128)} %adj_t.1, f32[32,32,128]{2,1,0:T(8,128)} %zonal.1, f32[32,32,128]{2,1,0:T(8,128)} %merid.1, f32[32]{0:T(128)} %cor.1, ...), custom_call_target="tpu_custom_call" | custom-call | tf_op jit(solution)/shard_map/adjoint/pallas_call | solution.py:713
  47.4 1.4 %store.1 = (f32[32,32,128]{2,1,0:T(8,128)}, f32[32,32,128]{2,1,0:T(8,128)}, f32[32,32,128]{2,1,0:T(8,128)}) custom-call(f32[32,32,128]{2,1,0:T(8,128)S(1)} %get-tuple-element.6.refs_0_, f32[32,32,128]{2,1,0:T(8,128)S(1)} %get-tuple-element.7.refs_1_, f32[32,32,128]{2,1,0:T(8,128)S(1)} %get-tuple-element.8.refs_2_), custom_call_target="tpu_custom_call" | custom-call | tf_op jit(solution)/shard_map/store/pallas_call | solution.py:762

commit v3 on v2

--- a/solution.py
+++ b/solution.py
@@ -452,44 +452,64 @@
     by_rows(
         2, 10, 1, lambda n: strip_block(n, lambda i, r: strips_own[i, 4 * n + r - HALO])
     )
-    def slope(kind, low, high, main, strip, main_out, strip_out, fold):
-        count = high - low
+    def slope(kind, ranges, main, strip, main_out, strip_out, fold):
+        at = [pl.ds(low, high - low) for low, high in ranges]
+        sizes = [high - low for low, high in ranges]
         got = jnp.dot(
-            split(strip(pl.ds(low, count)).reshape(8 * count, 128)),
+            jnp.concatenate([split(strip(a).reshape(8 * n, 128)) for a, n in zip(at, sizes)], axis=0),
             strip_mat[kind], preferred_element_type=F32,
         )
-        strip_out[pl.ds(low, count)] = got[:, :128].reshape(count, 8, 128)
-        edges = [
-            got[:, 128 * g + 128:128 * g + 256].reshape(count, 8, 128) for g in range(4)
-        ]
-        if not fold:
-            for g in range(4):
-                corr[g, pl.ds(low, count)] = edges[g]
-        parts = 4 if count > 8 else 1
-        part = count // parts
-        for n in range(parts):
-            at = pl.ds(low + part * n, part)
+        edges = []
+        start = 0
+        for a, n in zip(at, sizes):
+            mine = got[8 * start:8 * (start + n)]
+            start += n
+            strip_out[a] = mine[:, :128].reshape(n, 8, 128)
+            edges.append([
+                mine[:, 128 * g + 128:128 * g + 256].reshape(n, 8, 128) for g in range(4)
+            ])
+            if not fold:
+                for g in range(4):
+                    corr[g, a] = edges[-1][g]
+
+        def emit(a, out, mine):
+            if fold:
+                out = out + jnp.concatenate(mine, axis=1)
+            main_out[a] = out
+
+        if len(ranges) > 1:
             out = jnp.dot(
-                split(main(at).reshape(32 * part, 128)), main_mat[kind],
+                jnp.concatenate(
+                    [split(main(a).reshape(32 * n, 128)) for a, n in zip(at, sizes)], axis=0
+                ),
+                main_mat[kind], preferred_element_type=F32,
+            )
+            start = 0
+            for a, n, mine in zip(at, sizes, edges):
+                emit(a, out[32 * start:32 * (start + n)].reshape(n, 32, 128), mine)
+                start += n
+            return
+        part = sizes[0] // 4
+        for n in range(4):
+            a = pl.ds(ranges[0][0] + part * n, part)
+            out = jnp.dot(
+                split(main(a).reshape(32 * part, 128)), main_mat[kind],
                 preferred_element_type=F32,
             ).reshape(part, 32, 128)
-            if fold:
-                mine = [e[part * n:part * n + part] for e in edges]
-                out = out + jnp.concatenate(mine, axis=1)
-            main_out[at] = out
-
-    def fixed_slopes(low, high):
-        slope(1, low, high, lambda at: uu[at], lambda at: s_raw[UU, at], xu, s_xu, True)
+            emit(a, out, [e[part * n:part * n + part] for e in edges[0]])
+
+    def fixed_slopes(*ranges):
+        slope(1, ranges, lambda at: uu[at], lambda at: s_raw[UU, at], xu, s_xu, True)
         slope(
-            1, low, high, lambda at: 36.0 * mask[at] * raw[VV, at],
+            1, ranges, lambda at: 36.0 * mask[at] * raw[VV, at],
             lambda at: 36.0 * s_mask[at] * s_raw[VV, at], xv, s_xv, True,
         )
         slope(
-            1, low, high, lambda at: mask[at] * flat[1, at][:, None, :],
+            1, ranges, lambda at: mask[at] * flat[1, at][:, None, :],
             lambda at: s_mask[at] * flat_s[1, at][:, None, :], xb, s_xb, True,
         )
 
-    fixed_slopes(HALO, HALO + OWN)
+    fixed_slopes((HALO, HALO + OWN))
 
     finish(b_copies)
     ups = []
@@ -519,7 +539,7 @@
 
     by_rows(HALO, HALO + OWN, 4, lambda y: gradient(y, ups[0], HALO))
     def column(k, low, high, last, get, emit):
-        flux, held, vs = {}, {}, {}
+        flux, held, vs, power = {}, {}, {}, {}
 
         def reach(y):
             held[y] = get("t", y)
@@ -529,7 +549,8 @@
             if k == 0:
                 vs[y] = get("v", y)
             else:
-                vs[y] = row(coef, 2 * k, y) * get("v", y) + row(coef, 2 * k + 1, y) * get("u", y)
+                power[y] = row(coef, 2 * k, y), row(coef, 2 * k + 1, y)
+                vs[y] = power[y][0] * get("v", y) + power[y][1] * get("u", y)
 
         for y in range(low - 2, low + 2):
             reach(y)
@@ -542,9 +563,7 @@
             if k == 0:
                 z_x = z_x + get("xu", y)
             else:
-                z_x = z_x + (
-                    row(coef, 2 * k, y) * get("xu", y) - row(coef, 2 * k + 1, y) * get("xv", y)
-                )
+                z_x = z_x + (power[y][0] * get("xu", y) - power[y][1] * get("xv", y))
             z_y = 8.0 * (flux[y + 1] - flux[y - 1]) + (vs[y + 1] - vs[y - 1])
             z_y = z_y - (flux[y + 2] - flux[y - 2])
             scale = (1.0 / 12.0) if last else get("m", y)
@@ -552,11 +571,10 @@
 
     def step(k, ranges, last):
         now, new = k % 2, 1 - k % 2
-        for low, high in ranges:
-            slope(
-                0, low, high, lambda at: raw[U, at] * tr[now, at],
-                lambda at: s_raw[U, at] * s_tr[now, at], zx, corr.at[4], False,
-            )
+        slope(
+            0, ranges, lambda at: raw[U, at] * tr[now, at],
+            lambda at: s_raw[U, at] * s_tr[now, at], zx, corr.at[4], False,
+        )
 
         def strip_get(what, y):
             return {
@@ -594,7 +612,7 @@
                 column(k, low, high, last, get, emit)
             return c
 
-        lax.fori_loop(0, 4, group, 0)
+        lax.fori_loop(0, 4, group, 0, unroll=4)
 
     def inner_rows(k, last):
         for n in range(1, 5):
@@ -606,7 +624,7 @@
             step(k + n - 1, ((low, low + HALO), (high - HALO, high)), last and n == 4)
 
     inner_rows(0, False)
-    finish(late_copies)
+    finish(late_copies[:6])
     by_rows(0, HALO, 4, prepare_row)
     by_rows(HALO + OWN, ROWS, 4, prepare_row)
     for outer in (0, ROWS - 2):
@@ -614,16 +632,23 @@
     for outer in (0, ROWS - 1):
         raw[pl.ds(2, 2), outer] = jnp.zeros((2, 32, 128), F32)
 
-    def strip_outer(n):
-        return strip_block(
-            n, lambda i, r: pack([raw[i, 4 * n + r, pl.ds(8 * g, 8), :] for g in range(4)])
-        )
-
-    by_rows(0, 2, 1, strip_outer)
-    by_rows(10, 12, 1, strip_outer)
-
-    fixed_slopes(2, HALO)
-    fixed_slopes(HALO + OWN, ROWS - 2)
+    def pack_outer(shift):
+        return lambda n: [
+            (strips_own, (i, 4 * n + r + shift),
+             pack([raw[i, 4 * n + r, pl.ds(8 * g, 8), :] for g in range(4)]))
+            for r in range(4) for i in range(5)
+        ]
+
+    by_rows(0, 2, 1, pack_outer(OWN))
+    by_rows(10, 12, 1, pack_outer(0))
+    finish(late_copies[6:])
+    def strip_outer(shift):
+        return lambda n: strip_block(n, lambda i, r: strips_own[i, 4 * n + r + shift])
+
+    by_rows(0, 2, 1, strip_outer(OWN))
+    by_rows(10, 12, 1, strip_outer(0))
+
+    fixed_slopes((2, HALO), (HALO + OWN, ROWS - 2))
     by_rows(0, HALO, 4, lambda y: gradient(y, ups[1], HALO - OWN))
     by_rows(HALO + OWN, ROWS, 4, lambda y: gradient(y, ups[1], HALO + OWN))
     outer_rows(0, False)
@@ -719,7 +744,7 @@
             pltpu.VMEM((5, ROWS, 32, 128), F32),
             pltpu.VMEM((2, ROWS, 32, 128), F32),
             main, main, main,
-            pltpu.VMEM((5, OWN, 8, 128), F32),
+            pltpu.VMEM((5, ROWS, 8, 128), F32),
             pltpu.VMEM((2, 40, 8, 128), F32),
             pltpu.VMEM((60, 8, 128), F32),
             pltpu.VMEM((60, 8, 128), F32),

time: 48.9 us -> 43.7 us (0.89)
  Pallas kernels: 48.2 us -> 43 us
    pallas_call x1, Pallas kernels: 46.8 us -> 41.6 us  [per_device(): pl.pallas_call(kernel, out_shape=(held,) * 3, in_specs=[pl.BlockSpec(memo...]
where the time goes in v3:
time: 43.7 us; the launch traced here: 43.6 us
  Pallas kernels  43 us (98%)
  between operations  0.64 us (1%)
    pallas_call x1, Pallas kernels, per_device(): pl.pallas_call(kernel, out_shape=(held,) * 3, in_specs=[pl.BlockSpec(memo...  41.6 us
    pallas_call x1, Pallas kernels, per_device(): pl.pallas_call(store, out_shape=(jax.ShapeDtypeStruct((32, 32, 128), F32)...  1.36 us

profile of v3, /device:TPU:2, one launch (start us, length us, event | category | flops | bytes accessed | tf_op | source)
XLA Modules:
  0.0 43.6 jit_solution(6476615239196119319)
XLA Ops:
  0.6 41.6 %adjoint.1 = (f32[32,32,128]{2,1,0:T(8,128)S(1)}, f32[32,32,128]{2,1,0:T(8,128)S(1)}, f32[32,32,128]{2,1,0:T(8,128)S(1)}) custom-call(f32[32,32,128]{2,1,0:T(8,128)} %adj_u.1, f32[32,32,128]{2,1,0:T(8,128)} %adj_v.1, f32[32,32,128]{2,1,0:T(8,128)} %adj_t.1, f32[32,32,128]{2,1,0:T(8,128)} %zonal.1, f32[32,32,128]{2,1,0:T(8,128)} %merid.1, f32[32]{0:T(128)} %cor.1, ...), custom_call_target="tpu_custom_call" | custom-call | tf_op jit(solution)/shard_map/adjoint/pallas_call | solution.py:738
  42.2 1.4 %store.1 = (f32[32,32,128]{2,1,0:T(8,128)}, f32[32,32,128]{2,1,0:T(8,128)}, f32[32,32,128]{2,1,0:T(8,128)}) custom-call(f32[32,32,128]{2,1,0:T(8,128)S(1)} %get-tuple-element.6.refs_0_, f32[32,32,128]{2,1,0:T(8,128)S(1)} %get-tuple-element.7.refs_1_, f32[32,32,128]{2,1,0:T(8,128)S(1)} %get-tuple-element.8.refs_2_), custom_call_target="tpu_custom_call" | custom-call | tf_op jit(solution)/shard_map/store/pallas_call | solution.py:787
